TPU v7x, 32 devices: a whole 2x2x4 slice. The times are simulated.
32 devices in a mesh: row: 4 (over z), col: 8 (over y, x, core).
Axes of the slice: x: 2, y: 2, z: 4, core: 2. Of those that a mesh axis runs over, the one named last changes fastest.
Arguments:
- counts: int32 [8192, 16384], P('row', 'col'), may hold values from 0 to 512
- block_mask: int32 [32, 64], P('row', 'col'), may hold values from 0 to 1
- row_perm: int32 [8192], P('row'), may hold values from 0 to 8191, as said below
- col_perm: int32 [16384], P('col'), may hold values from 0 to 16383, as said below
- row_logm: float32 [8192], P('row'), may hold values from 0 to 3
- col_logm: float32 [16384], P('col'), may hold values from 0 to 3
- row_emb: bfloat16 [8192, 512], P(('row', 'col')), may hold values from -1.1953125 to 1.1953125
- col_emb: bfloat16 [16384, 512], P(('col', 'row')), may hold values from -1.1953125 to 1.1953125
Outputs:
- row_grad: float32 [8192, 512], P(('row', 'col'))
- col_grad: float32 [16384, 512], P(('col', 'row'))
Inputs may be any that keep to these rules, and one draw needn't show every extreme that they name: `row_perm`: each aligned block of 2048 entries is a permutation of that block's own index range. `col_perm`: each aligned block of 2048 entries is a permutation of that block's own index range.
All inputs are finite; a program needn't handle non-finite values.
Results may differ from a plain program's by a relative error of at most 0.0022.
Values may be sent and summed in bfloat16 or wider, within the bound.
No kernel may reach another device: no remote copies, remote signals or barrier semaphores. Data moves between devices by JAX's collectives and lax.ppermute only.
A program may use at most 128 MiB of HBM per device.

v0:
```python
import jax
import jax.numpy as jnp
from jax import lax
from jax.sharding import PartitionSpec as P


def cell_delta(score, count, active, row_part, col_part):
    real_count = count.astype(jnp.float32)
    safe = jnp.maximum(real_count, 1.0)
    pmi = jnp.log(safe) - row_part[:, None] - col_part[None, :]
    confid = 0.1 + 0.25 * jnp.sqrt(safe)
    positive = confid * (score - pmi)
    zeroed = jax.nn.sigmoid(score - pmi)
    deriv = jnp.where(count > 0, positive, zeroed)
    return (active.astype(jnp.float32) * deriv).astype(jnp.bfloat16)


def shards(counts, block_mask, row_perm, col_perm, row_logm, col_logm, row_emb, col_emb):
    shard_rows = counts.shape[0]
    shard_cols = counts.shape[1]
    all_cols = shard_cols * lax.axis_size("col")
    all_rows = shard_rows * lax.axis_size("row")
    block_side = shard_rows // block_mask.shape[0]
    row_group = lax.all_gather(row_emb, "col", axis=0, tiled=True)
    col_group = lax.all_gather(col_emb, "row", axis=0, tiled=True)
    row_local = row_perm - lax.axis_index("row") * shard_rows
    col_local = col_perm - lax.axis_index("col") * shard_cols
    wvec = jnp.take(row_group, row_local, axis=0)
    cvec = jnp.take(col_group, col_local, axis=0)
    score = lax.dot_general(
        wvec, cvec, (((1,), (1,)), ((), ())), preferred_element_type=jnp.float32
    )
    active = jnp.repeat(jnp.repeat(block_mask, block_side, axis=0), block_side, axis=1)
    delta = cell_delta(score, counts, active, row_logm, col_logm)
    row_scale = 1.0 / jnp.sqrt(jnp.float32(all_cols))
    col_scale = 1.0 / jnp.sqrt(jnp.float32(all_rows))
    gshard = jnp.dot(delta, cvec, preferred_element_type=jnp.float32) * row_scale
    ordered = jnp.zeros(gshard.shape, jnp.float32).at[row_local].set(gshard)
    row_grad = lax.psum_scatter(ordered, "col", scatter_dimension=0, tiled=True)
    hshard = (
        lax.dot_general(delta, wvec, (((0,), (0,)), ((), ())), preferred_element_type=jnp.float32)
        * col_scale
    )
    col_ordered = jnp.zeros(hshard.shape, jnp.float32).at[col_local].set(hshard)
    col_grad = lax.psum_scatter(col_ordered, "row", scatter_dimension=0, tiled=True)
    return (row_grad, col_grad)


def solution(mesh):
    in_specs = (
        P("row", "col"),
        P("row", "col"),
        P("row"),
        P("col"),
        P("row"),
        P("col"),
        P(("row", "col"), None),
        P(("col", "row"), None),
    )
    out_specs = (P(("row", "col"), None), P(("col", "row"), None))
    return jax.shard_map(shards, mesh=mesh, in_specs=in_specs, out_specs=out_specs, check_vma=False)
```

profile of v0, /device:TPU:0, one launch (start us, length us, event | category | flops | bytes accessed | tf_op | source)
XLA Modules:
  0.0 280.6 jit_solution(5450672202295521951)
XLA Ops:
  7.2 0.0 all-gather.5.cloned.1.call-start
  7.2 0.7 all-gather.5.cloned.1.call-update
  7.9 0.0 all-gather.3.cloned.1.call-start
  7.9 0.7 all-gather.3.cloned.1.call-update
  8.6 0.0 reduce-scatter.3.cloned.1.call-start
  8.7 0.7 convert_element_type.17
  9.4 0.1 broadcast_in_dim.24
  9.5 2.5 broadcast_in_dim.25
  11.9 0.0 copy-start.1
  11.9 0.0 copy-start.2
  11.9 11.2 %copy.10 = f32[256,8,8,256]{3,1,2,0:T(8,128)} copy(f32[256,8,8,256]{3,2,1,0:T(8,128)S(1)} %bitcast.5) | data formatting | bytes 33554432
  23.2 0.0 copy-done.1
  23.2 0.0 copy-done.2
  23.2 35.0 %all-gather.5.cloned.1.call-done = bf16[2048,512]{1,0:T(8,128)(2,1)} async-done(((bf16[512,512]{1,0:T(8,128)(2,1)}), bf16[2048,512]{1,0:T(8,128)(2,1)}) %all-gather.5.cloned.1.call-update) | async-done | bytes 2097168 | tf_op jit(solution)/shard_map/all_gather | solution.py:25
  58.2 11.1 %gather_fusion.1 = bf16[2048,512]{1,0:T(8,128)(2,1)} fusion(bf16[2048,512]{1,0:T(8,128)(2,1)} %all-gather.5.cloned.1.call-done, s32[2048]{0:T(1024)S(1)} %broadcast_clamp_fusion), kind=kCustom, calls=%fused_computation.1.clone | custom fusion | bytes 4202496 | tf_op jit(solution)/shard_map/jit(_take)/gather | solution.py:29
  69.4 0.0 copy-start.3
  69.4 0.0 copy-start.4
  69.4 17.4 %all-gather.3.cloned.1.call-done = bf16[2048,512]{1,0:T(8,128)(2,1)} async-done(((bf16[256,512]{1,0:T(8,128)(2,1)}), bf16[2048,512]{1,0:T(8,128)(2,1)}) %all-gather.3.cloned.1.call-update) | async-done | bytes 2097168 | tf_op jit(solution)/shard_map/all_gather | solution.py:24
  86.8 9.4 %gather_fusion = bf16[2048,512]{1,0:T(8,128)(2,1)S(1)} fusion(bf16[2048,512]{1,0:T(8,128)(2,1)} %all-gather.3.cloned.1.call-done, s32[2048]{0:T(1024)S(1)} %broadcast_clamp_fusion.1), kind=kCustom, calls=%fused_computation.clone | custom fusion | bytes 4202496 | tf_op jit(solution)/shard_map/jit(_take)/gather | solution.py:28
  96.2 0.0 copy-done.3
  96.2 0.0 copy-done.4
  96.2 0.0 copy-start
  96.3 24.6 %multiply_convert_fusion = bf16[2048,2048]{1,0:T(8,128)(2,1)} fusion(f32[2048,2048]{1,0:T(8,128)} %bitcast.6, s32[2048,2048]{1,0:T(8,128)} %param.10, f32[2048]{0:T(1024)S(1)} %copy-done.3, f32[2048]{0:T(1024)S(1)} %copy-done.4, bf16[2048,512]{1,0:T(8,128)(2,1)S(1)} %gather_fusion, pred[2048]{0:T(1024)(128)(4,1)S(1)} %get-tuple-element.7, ...), kind=kOutput, calls=%fused_computation.4 | convolution fusion | flops 4359979008 | bytes 46157824 | tf_op jit(solution)/shard_map/dot_general | solution.py:30
  120.9 0.0 copy-done
  120.9 10.0 %fusion.9 = f32[2048,512]{1,0:T(8,128)} fusion(bf16[2048,2048]{1,0:T(8,128)(2,1)} %multiply_convert_fusion, bf16[2048,512]{1,0:T(8,128)(2,1)S(1)} %copy-done, pred[2048]{0:T(1024)(128)(4,1)S(1)} %get-tuple-element.3), kind=kOutput, calls=%fused_computation.16 | convolution fusion | flops 4296015872 | bytes 14682112 | tf_op jit(solution)/shard_map/dot_general | solution.py:37
  130.8 12.1 %scatter_custom_fusion = f32[2048,512]{1,0:T(8,128)} fusion(s32[2048]{0:T(1024)S(1)} %get-tuple-element.8, f32[2048,512]{1,0:T(8,128)} %fusion.9, f32[]{:T(128)} %constant.10.clone.1, f32[]{:T(128)} %constant.18.clone.1), kind=kCustom, calls=%fused_computation.7 | custom fusion | flops 1048576 | bytes 8388616 | tf_op jit(solution)/shard_map/scatter | solution.py:38
  142.9 0.0 reduce-scatter.3.cloned.1.call-update
  142.9 0.0 reduce-scatter.5.cloned.1.call-start
  143.0 10.0 %fusion.8 = f32[2048,512]{1,0:T(8,128)} fusion(bf16[2048,2048]{1,0:T(8,128)(2,1)} %multiply_convert_fusion, bf16[2048,512]{1,0:T(8,128)(2,1)S(1)} %gather_fusion, pred[2048]{0:T(1024)(128)(4,1)S(1)} %get-tuple-element.7), kind=kOutput, calls=%fused_computation.15 | convolution fusion | flops 4296015872 | bytes 14682112 | tf_op jit(solution)/shard_map/dot_general | solution.py:41
  153.0 12.4 %scatter_custom_fusion.1 = f32[2048,512]{1,0:T(8,128)} fusion(s32[2048]{0:T(1024)S(1)} %get-tuple-element.4, f32[2048,512]{1,0:T(8,128)} %fusion.8, f32[]{:T(128)} %constant.15.clone.1, f32[]{:T(128)} %constant.18.clone.1), kind=kCustom, calls=%fused_computation.5 | custom fusion | flops 1048576 | bytes 8388616 | tf_op jit(solution)/shard_map/scatter | solution.py:44
  165.4 0.0 reduce-scatter.5.cloned.1.call-update
  165.4 29.0 %reduce-scatter.3.cloned.1.call-done = f32[256,512]{1,0:T(8,128)} async-done(((f32[2048,512]{1,0:T(8,128)}), f32[256,512]{1,0:T(8,128)}) %reduce-scatter.3.cloned.1.call-update) | async-done | bytes 524304 | tf_op jit(solution)/shard_map/reduce_scatter | solution.py:39
  194.4 79.6 %reduce-scatter.5.cloned.1.call-done = f32[512,512]{1,0:T(8,128)} async-done(((f32[2048,512]{1,0:T(8,128)}), f32[512,512]{1,0:T(8,128)}) %reduce-scatter.5.cloned.1.call-update) | async-done | bytes 1048592 | tf_op jit(solution)/shard_map/reduce_scatter | solution.py:45
  (3 shorter events, 0.0 us)
Async XLA Ops:
  7.2 51.1 %all-gather.5.cloned.1.call-start = ((), (), s32[]{:S(2)}) async-start(), calls=%async_computation.3 | async-start | bytes 2621440 | tf_op jit(solution)/shard_map/all_gather | solution.py:25
  7.9 78.9 %all-gather.3.cloned.1.call-start = ((), (), s32[]{:S(2)}) async-start(), calls=%async_computation.2 | async-start | bytes 2359296 | tf_op jit(solution)/shard_map/all_gather | solution.py:24
  8.6 185.8 %reduce-scatter.3.cloned.1.call-start = ((), (), s32[]{:S(2)}) async-start(), calls=%async_computation.4 | async-start | bytes 4718592 | tf_op jit(solution)/shard_map/reduce_scatter | solution.py:39
  11.9 11.2 %copy-start.1 = (s32[2048]{0:T(1024)S(1)}, s32[2048]{0:T(1024)}, u32[]{:S(2)}) copy-start(s32[2048]{0:T(1024)} %param.13) | copy-start | bytes 24580
  11.9 11.2 %copy-start.2 = (s32[2048]{0:T(1024)S(1)}, s32[2048]{0:T(1024)}, u32[]{:S(2)}) copy-start(s32[2048]{0:T(1024)} %param.12) | copy-start | bytes 24580
  69.4 26.9 %copy-start.3 = (f32[2048]{0:T(1024)S(1)}, f32[2048]{0:T(1024)}, u32[]{:S(2)}) copy-start(f32[2048]{0:T(1024)} %param.15) | copy-start | bytes 24580
  69.4 26.9 %copy-start.4 = (f32[2048]{0:T(1024)S(1)}, f32[2048]{0:T(1024)}, u32[]{:S(2)}) copy-start(f32[2048]{0:T(1024)} %param.14) | copy-start | bytes 24580
  96.2 24.6 %copy-start = (bf16[2048,512]{1,0:T(8,128)(2,1)S(1)}, bf16[2048,512]{1,0:T(8,128)(2,1)}, u32[]{:S(2)}) copy-start(bf16[2048,512]{1,0:T(8,128)(2,1)} %gather_fusion.1) | copy-start | bytes 6291460
  142.9 131.1 %reduce-scatter.5.cloned.1.call-start = ((), (), s32[]{:S(2)}) async-start(), calls=%async_computation.5 | async-start | bytes 5242880 | tf_op jit(solution)/shard_map/reduce_scatter | solution.py:45
Sparse Core Ops, SparseCore 0:
  9.6 48.6 all-gather.4
  60.1 26.5 all-gather.2
  143.1 51.3 reduce-scatter.2
  197.2 76.7 reduce-scatter.4
where the time goes:
time: 281 us
  waiting for transfers between devices  162 us (58%)
  matrix products  44.6 us (16%)
  local copies, waits for them, and re-layouts  34.4 us (12%)
  other arithmetic  25.2 us (9%)
  between operations  13.8 us (5%)
    reduce_scatter x1, waiting for transfers between devices, shards(): lax.psum_scatter(col_ordered, 'row', scatter_dimension=0, tiled=True)  79.6 us
    all_gather x1, waiting for transfers between devices, shards(): col_group = lax.all_gather(col_emb, 'row', axis=0, tiled=True)  35 us
    reduce_scatter x1, waiting for transfers between devices, shards(): row_grad = lax.psum_scatter(ordered, 'col', scatter_dimension=0, tiled=True)  29 us
    dot_general x1, matrix products, shards(): lax.dot_general(wvec, cvec, (((1,), (1,)), ((), ())), preferred_element_t...  24.6 us
    all_gather x1, waiting for transfers between devices, shards(): row_group = lax.all_gather(row_emb, 'col', axis=0, tiled=True)  17.4 us
    scatter x1, other arithmetic, shards(): col_ordered = jnp.zeros(hshard.shape, jnp.float32).at[col_local].set(hshard)  12.4 us
    scatter x1, other arithmetic, shards(): ordered = jnp.zeros(gshard.shape, jnp.float32).at[row_local].set(gshard)  12.1 us
    unnamed x11, local copies, waits for them, and re-layouts  11.2 us
  transfers between devices with their start and end apart: 4, of which 4 were waited for; matrix products, arithmetic and copies ran while one was open for 17% of the time, Pallas kernels for 0%

commit v1 on v0

v1 whole, which is shorter than its diff:
```python
import functools

import jax
import jax.numpy as jnp
import numpy as np
from jax import lax
from jax.experimental import pallas as pl
from jax.experimental.pallas import tpu as pltpu
from jax.sharding import PartitionSpec as P

F32 = jnp.float32
BF16 = jnp.bfloat16
LANES = 128
MIB = 1 << 20


def cell_delta(score, count, active, row_part, col_part):
    real_count = count.astype(F32)
    safe = jnp.maximum(real_count, 1.0)
    pmi = jnp.log(safe) - row_part[:, None] - col_part[None, :]
    confid = 0.1 + 0.25 * jnp.sqrt(safe)
    positive = confid * (score - pmi)
    zeroed = jax.nn.sigmoid(score - pmi)
    deriv = jnp.where(count > 0, positive, zeroed)
    return (active.astype(F32) * deriv).astype(BF16)


def plain_shards(counts, block_mask, row_perm, col_perm, row_logm, col_logm, row_emb, col_emb):
    shard_rows, shard_cols = counts.shape
    all_cols = shard_cols * lax.axis_size("col")
    all_rows = shard_rows * lax.axis_size("row")
    block_side = shard_rows // block_mask.shape[0]
    row_group = lax.all_gather(row_emb, "col", axis=0, tiled=True)
    col_group = lax.all_gather(col_emb, "row", axis=0, tiled=True)
    row_local = row_perm - lax.axis_index("row") * shard_rows
    col_local = col_perm - lax.axis_index("col") * shard_cols
    wvec = jnp.take(row_group, row_local, axis=0)
    cvec = jnp.take(col_group, col_local, axis=0)
    score = lax.dot_general(wvec, cvec, (((1,), (1,)), ((), ())), preferred_element_type=F32)
    active = jnp.repeat(jnp.repeat(block_mask, block_side, axis=0), block_side, axis=1)
    delta = cell_delta(score, counts, active, row_logm, col_logm)
    gshard = jnp.dot(delta, cvec, preferred_element_type=F32) / jnp.sqrt(F32(all_cols))
    ordered = jnp.zeros(gshard.shape, F32).at[row_local].set(gshard)
    row_grad = lax.psum_scatter(ordered, "col", scatter_dimension=0, tiled=True)
    hshard = lax.dot_general(
        delta, wvec, (((0,), (0,)), ((), ())), preferred_element_type=F32
    ) / jnp.sqrt(F32(all_rows))
    col_ordered = jnp.zeros(hshard.shape, F32).at[col_local].set(hshard)
    col_grad = lax.psum_scatter(col_ordered, "row", scatter_dimension=0, tiled=True)
    return (row_grad, col_grad)


def params(mib):
    return pltpu.CompilerParams(vmem_limit_bytes=mib * MIB)


def cost(flops, moved, trans=0):
    return pl.CostEstimate(flops=flops, bytes_accessed=moved, transcendentals=trans)


def onehot(flag):
    return jnp.where(flag, 1.0, 0.0).astype(BF16)


def pieces_of(value):
    high = value.astype(BF16)
    rest = value - high.astype(F32)
    middle = rest.astype(BF16)
    low = (rest - middle.astype(F32)).astype(BF16)
    return high, middle, low


def order_kernel(width, parts, base_ref, index_ref, aux_ref, count_ref, out_ref, aux_out_ref, pick):
    @pl.when(pl.program_id(0) == 0)
    def _():
        index = index_ref[...].T
        depth = pick.shape[0]
        lane = lax.broadcasted_iota(jnp.int32, (LANES, width), 1)
        for part in range(parts):
            vocab = (lane + base_ref[part] * width).astype(F32)
            for group in range(depth // LANES):
                pick[pl.ds(group * LANES, LANES), pl.ds(part * width, width)] = onehot(
                    index[:, group : group + 1] == vocab
                )
        aux = jnp.concatenate(pieces_of(aux_ref[...]), axis=0)
        moved = jnp.dot(aux, pick[...], preferred_element_type=F32)
        rows = aux_ref.shape[0]
        aux_out_ref[...] = moved[:rows] + moved[rows : 2 * rows] + moved[2 * rows :]

    shifted = (count_ref[...].astype(F32) - 256.0).astype(BF16)
    out_ref[...] = jnp.dot(shifted, pick[...], preferred_element_type=F32).astype(BF16)


def order_counts(counts, index, aux, bases, width):
    rows, cols = counts.shape
    parts = bases.shape[0]
    step = 512
    grid_spec = pltpu.PrefetchScalarGridSpec(
        num_scalar_prefetch=1,
        grid=(rows // step,),
        in_specs=[
            pl.BlockSpec((LANES, LANES), lambda i, s: (0, 0)),
            pl.BlockSpec(aux.shape, lambda i, s: (0, 0)),
            pl.BlockSpec((step, cols), lambda i, s: (i, 0)),
        ],
        out_specs=[
            pl.BlockSpec((step, parts * width), lambda i, s: (i, 0)),
            pl.BlockSpec((aux.shape[0], parts * width), lambda i, s: (0, 0)),
        ],
        scratch_shapes=[pltpu.VMEM((cols, parts * width), BF16)],
    )
    return pl.pallas_call(
        functools.partial(order_kernel, width, parts),
        grid_spec=grid_spec,
        out_shape=[
            jax.ShapeDtypeStruct((rows, parts * width), BF16),
            jax.ShapeDtypeStruct((aux.shape[0], parts * width), F32),
        ],
        compiler_params=params(48),
        cost_estimate=cost(2 * rows * cols * parts * width, 4 * rows * cols),
        name="order_counts",
    )(bases, index, aux, counts)


def rows_kernel(index_ref, *refs):
    blocks, (out_ref, logm_ref, group, pick) = refs[:-4], refs[-4:]
    side = blocks[0].shape[0]
    for at, block in enumerate(blocks):
        group[pl.ds(at * side, side), :] = block[...]
    index = index_ref[...].T
    rows = out_ref.shape[0]
    depth = group.shape[0]
    step = pick.shape[0]
    vocab = lax.broadcasted_iota(jnp.int32, (LANES, depth), 1).astype(F32)
    for first in range(0, rows, step):
        for inner in range(0, step, LANES):
            at = (first + inner) // LANES
            column = rows // LANES + at
            pick[pl.ds(inner, LANES), :] = onehot(index[:, column : column + 1] == vocab)
            column = 2 * (rows // LANES) + at
            logm_ref[pl.ds(first + inner, LANES), :] = jnp.broadcast_to(
                index[:, column : column + 1], (LANES, LANES)
            )
        out_ref[pl.ds(first, step), :] = jnp.dot(
            pick[...], group[...], preferred_element_type=F32
        ).astype(BF16)


def take_rows(index, blocks, rows):
    side, width = blocks[0].shape
    depth = side * len(blocks)
    return pl.pallas_call(
        rows_kernel,
        out_shape=[
            jax.ShapeDtypeStruct((rows, width), BF16),
            jax.ShapeDtypeStruct((rows, LANES), F32),
        ],
        scratch_shapes=[pltpu.VMEM((depth, width), BF16), pltpu.VMEM((512, depth), BF16)],
        compiler_params=params(32),
        cost_estimate=cost(2 * rows * depth * width, 4 * rows * width),
        name="take_rows",
    )(index, *blocks)


def cells_kernel(has_sum, pick_ref, first_ref, second_ref, wvec_ref, count_ref, aux_ref, logm_ref, *refs):
    if has_sum:
        before_ref, refs = refs[0], refs[1:]
    grad_ref, term_ref, sent_ref, chunk = refs
    step_at = pl.program_id(0)

    @pl.when(step_at == 0)
    def _():
        @pl.when(pick_ref[0] == 1)
        def _():
            chunk[...] = first_ref[...]

        @pl.when(pick_ref[0] == 0)
        def _():
            chunk[...] = second_ref[...]

    cvec = chunk[...]
    width = cvec.shape[0]
    side = 256
    halves = wvec_ref.shape[0] // side
    col_logm = aux_ref[8:9, :]
    total = None
    for half in range(halves):
        here = pl.ds(half * side, side)
        wvec = wvec_ref[here, :]
        score = lax.dot_general(wvec, cvec, (((1,), (1,)), ((), ())), preferred_element_type=F32)
        count = count_ref[here, :].astype(F32) + 256.0
        safe = jnp.maximum(count, 1.0)
        row_logm = jnp.concatenate([logm_ref[here, :]] * (width // LANES), axis=1)
        gap = score + ((row_logm + col_logm) - jnp.log(safe))
        confid = 0.1 + 0.25 * (safe * lax.rsqrt(safe))
        zeroed = 0.5 * jnp.tanh(0.5 * gap) + 0.5
        deriv = jnp.where(count > 0.0, confid * gap, zeroed)
        active = aux_ref[pl.ds(step_at * halves + half, 1), :]
        delta = (deriv * active).astype(BF16)
        grad = jnp.dot(delta, cvec, preferred_element_type=F32)
        if has_sum:
            grad = grad + before_ref[here, :]
        grad_ref[here, :] = grad
        term = lax.dot_general(delta, wvec, (((0,), (0,)), ((), ())), preferred_element_type=F32)
        total = term if total is None else total + term

    @pl.when(step_at == 0)
    def _():
        term_ref[...] = total

    @pl.when(step_at > 0)
    def _():
        term_ref[...] += total

    @pl.when(step_at == pl.num_programs(0) - 1)
    def _():
        sent_ref[...] = term_ref[...].astype(BF16)


def cells(pick, first, second, wvec, ordered, aux, at, logm, before):
    rows, depth = wvec.shape
    width = first.shape[0]
    step = 512
    whole = lambda i, s: (0, 0)
    block = lambda i, s: (i, 0)
    in_specs = [
        pl.BlockSpec((width, depth), whole),
        pl.BlockSpec((width, depth), whole),
        pl.BlockSpec((step, depth), block),
        pl.BlockSpec((step, width), lambda i, s: (i, at)),
        pl.BlockSpec((aux.shape[0], width), lambda i, s: (0, at)),
        pl.BlockSpec((step, LANES), block),
    ]
    args = [pick, first, second, wvec, ordered, aux, logm]
    aliases = {}
    if before is not None:
        in_specs.append(pl.BlockSpec((step, depth), block))
        aliases = {len(args): 0}
        args.append(before)
    grid_spec = pltpu.PrefetchScalarGridSpec(
        num_scalar_prefetch=1,
        grid=(rows // step,),
        in_specs=in_specs,
        out_specs=[
            pl.BlockSpec((step, depth), block),
            pl.BlockSpec((width, depth), whole),
            pl.BlockSpec((width, depth), whole),
        ],
        scratch_shapes=[pltpu.VMEM((width, depth), BF16)],
    )
    return pl.pallas_call(
        functools.partial(cells_kernel, before is not None),
        grid_spec=grid_spec,
        out_shape=[
            jax.ShapeDtypeStruct((rows, depth), F32),
            jax.ShapeDtypeStruct((width, depth), F32),
            jax.ShapeDtypeStruct((width, depth), BF16),
        ],
        input_output_aliases=aliases,
        compiler_params=params(32),
        cost_estimate=cost(6 * rows * width * depth, 12 * MIB, 3 * rows * width),
        name="cells",
    )(*args)


def put_kernel(first, index_ref, grad_ref, out_ref):
    grad = grad_ref[...]
    high = grad.astype(BF16)
    low = (grad - high.astype(F32)).astype(BF16)
    both = jnp.concatenate([high, low], axis=1)
    width = grad.shape[1]
    blocks, side = out_ref.shape[0], out_ref.shape[1]
    vocab = lax.broadcasted_iota(jnp.int32, (side, grad.shape[0]), 0)
    for at in range(blocks):
        pick = onehot(index_ref[...] == (vocab + (first + at) * side).astype(F32))
        moved = jnp.dot(pick, both, preferred_element_type=F32)
        out_ref[at] = moved[:, :width] + moved[:, width:]


def put_rows(index, grad, first, blocks, side):
    rows, width = grad.shape
    return pl.pallas_call(
        functools.partial(put_kernel, first),
        out_shape=jax.ShapeDtypeStruct((blocks, side, width), F32),
        compiler_params=params(32),
        cost_estimate=cost(4 * rows * blocks * side * width, 6 * rows * width),
        name="put_rows",
    )(index, grad)


def swap(value, axis, pairs):
    return lax.ppermute(value, axis, pairs)


def line_shards(counts, block_mask, row_perm, col_perm, row_logm, col_logm, row_emb, col_emb):
    shard_rows, shard_cols = counts.shape
    row_at = lax.axis_index("row")
    col_at = lax.axis_index("col")
    side = row_emb.shape[0]
    width = col_emb.shape[0]
    block_side = shard_rows // block_mask.shape[0]

    outward = [(1, 0), (2, 3)]
    inward = [(0, 1), (3, 2)]
    across = [(1, 2), (2, 1)]
    flip = lambda bit: [(i, i ^ bit) for i in range(8)]

    near = swap(col_emb, "row", outward + inward)
    over = swap(col_emb, "row", across)
    row_x = swap(row_emb, "col", flip(2))
    row_y = swap(row_emb, "col", flip(4))
    row_xy = swap(row_emb, "col", flip(6))
    mine = [row_emb, row_x, row_y, row_xy]
    other = [swap(block, "col", flip(1)) for block in mine]
    two_out = swap(over, "row", outward)
    far_over = swap(near, "row", across)
    three_out = swap(far_over, "row", outward)

    row_local = row_perm - row_at * shard_rows
    col_local = col_perm - col_at * shard_cols
    gap = (row_local // side) ^ col_at
    row_slot = ((gap >> 1) + 4 * (gap & 1)) * side + row_local % side
    row_index = row_slot.astype(F32)
    index = jnp.concatenate(
        [col_local.astype(F32), row_index, row_logm, jnp.zeros((LANES * LANES - 3 * shard_rows,), F32)]
    ).reshape(LANES, LANES)
    active = jnp.repeat(block_mask.astype(F32), block_side, axis=1)
    aux = jnp.concatenate([active, col_logm[None, :], jnp.zeros((7, shard_cols), F32)], axis=0)

    end = (row_at == 0) | (row_at == 3)
    real = lambda m: jnp.where(row_at >= 2, 3 - m, m)
    order = [real(jnp.where(end, e, m)) for e, m in ((1, 2), (2, 0), (3, 3), (0, 1))]
    order = [o.astype(jnp.int32) for o in order]
    at_end = end.astype(jnp.int32).reshape(1)

    early, aux_early = order_counts(counts, index, aux, jnp.stack(order[:2]), width)
    late, aux_late = order_counts(counts, index, aux, jnp.stack(order[2:]), width)
    wvec, logm = take_rows(index, mine + other, shard_rows)

    work = functools.partial(cells, at_end)
    grad, term_a, sent_a = work(near, over, wvec, early, aux_early, 0, logm, None)
    got_1 = swap(sent_a, "row", inward)
    grad, term_b, sent_b = work(two_out, near, wvec, early, aux_early, 1, logm, grad)
    got_2 = swap(sent_b, "row", inward)
    grad, term_c, sent_c = work(three_out, far_over, wvec, late, aux_late, 0, logm, grad)
    got_3 = swap(sent_c, "row", inward)
    grad, term_d, _ = work(col_emb, col_emb, wvec, late, aux_late, 1, logm, grad)

    sum_2 = (term_a + got_2.astype(F32)).astype(BF16)
    got_4 = swap(sum_2, "row", across)
    sum_3 = (term_c + got_3.astype(F32)).astype(BF16)
    got_5 = swap(sum_3, "row", across)
    sum_0 = (term_b + got_5.astype(F32)).astype(BF16)
    got_6 = swap(sum_0, "row", outward)
    col_sum = term_d + got_1.astype(F32) + got_4.astype(F32) + got_6.astype(F32)
    col_scale = np.float32(1.0 / np.sqrt(shard_rows * 4))
    col_grad = col_sum * col_scale

    row_line = row_index[None, :]
    away = put_rows(row_line, grad, 4, 4, side)
    home = put_rows(row_line, grad, 0, 4, side)
    core = swap(away, "col", flip(1))
    both = home + core
    sent = both[1:].astype(BF16)
    got_x = swap(sent[0], "col", flip(2))
    got_y = swap(sent[1], "col", flip(4))
    got_xy = swap(sent[2], "col", flip(6))
    row_scale = np.float32(1.0 / np.sqrt(shard_cols * 8))
    row_sum = both[0] + got_x.astype(F32) + got_y.astype(F32) + got_xy.astype(F32)
    return (row_sum * row_scale, col_grad)


def solution(mesh):
    in_specs = (
        P("row", "col"),
        P("row", "col"),
        P("row"),
        P("col"),
        P("row"),
        P("col"),
        P(("row", "col"), None),
        P(("col", "row"), None),
    )
    out_specs = (P(("row", "col"), None), P(("col", "row"), None))
    line = mesh.shape["row"] == 4 and mesh.shape["col"] == 8
    body = line_shards if line else plain_shards
    return jax.shard_map(body, mesh=mesh, in_specs=in_specs, out_specs=out_specs, check_vma=False)
```

time: 281 us -> 147 us (0.52)
  waiting for transfers between devices: 162 us -> 37.3 us
  Pallas kernels: 0 us -> 71.4 us
  matrix products: 44.6 us -> 0 us
  local copies, waits for them, and re-layouts: 34.4 us -> 5.94 us
  starting transfers between devices: 0.16 us -> 24.5 us
  other arithmetic: 25.2 us -> 6.32 us
  between operations: 13.8 us -> 0.94 us
    reduce_scatter x2 -> x0, waiting for transfers between devices: 109 us -> none  [the longest x1 79.6 us: shards(): lax.psum_scatter(col_ordered, 'row', scatter_dimension=0, tiled=True)]
    pallas_call x0 -> x9, Pallas kernels: none -> 71.4 us  [the longest x4 29.5 us: cells(): pl.pallas_call(functools.partial(cells_kernel, before is not None), grid_...]
    all_gather x2 -> x0, waiting for transfers between devices: 52.4 us -> none  [the longest x1 35 us: shards(): col_group = lax.all_gather(col_emb, 'row', axis=0, tiled=True)]
    dot_general x3 -> x0, matrix products: 44.6 us -> none  [the longest x1 24.6 us: shards(): lax.dot_general(wvec, cvec, (((1,), (1,)), ((), ())), preferred_element_t...]
    ppermute x0 -> x22, waiting for transfers between devices: none -> 37.3 us  [swap(): return lax.ppermute(value, axis, pairs)]
    ppermute x0 -> x22, starting transfers between devices: none -> 24.5 us  [swap(): return lax.ppermute(value, axis, pairs)]
    scatter x2 -> x0, other arithmetic: 24.5 us -> none  [the longest x1 12.4 us: shards(): col_ordered = jnp.zeros(hshard.shape, jnp.float32).at[col_local].set(hshard)]
    gather x2 -> x0, local copies, waits for them, and re-layouts: 20.6 us -> none  [the longest x1 11.1 us: shards(): cvec = jnp.take(col_group, col_local, axis=0)]
  transfers between devices with their start and end apart: 4 -> 22, of which waited for: 4 -> 6; matrix products, arithmetic and copies ran while one was open for 17% -> 4% of each run, Pallas kernels for 0% -> 35%
where the time goes in v1:
time: 147 us; the launch traced here: 146 us
  Pallas kernels  71.4 us (49%)
  waiting for transfers between devices  37.3 us (25%)
  starting transfers between devices  24.5 us (17%)
  other arithmetic  6.32 us (4%)
  local copies, waits for them, and re-layouts  5.94 us (4%)
    ppermute x22, waiting for transfers between devices, swap(): return lax.ppermute(value, axis, pairs)  37.3 us
    pallas_call x4, Pallas kernels, cells(): pl.pallas_call(functools.partial(cells_kernel, before is not None), grid_...  29.5 us
    pallas_call x2, Pallas kernels, order_counts(): pl.pallas_call(functools.partial(order_kernel, width, parts), grid_spec=g...  27 us
    ppermute x22, starting transfers between devices, swap(): return lax.ppermute(value, axis, pairs)  24.5 us
    pallas_call x2, Pallas kernels, put_rows(): pl.pallas_call(functools.partial(put_kernel, first), out_shape=jax.ShapeD...  9.25 us
    pallas_call x1, Pallas kernels, take_rows(): pl.pallas_call(rows_kernel, out_shape=[jax.ShapeDtypeStruct((rows, width)...  5.71 us
    unnamed x16, local copies, waits for them, and re-layouts  5.66 us
  transfers between devices with their start and end apart: 22, of which 6 were waited for; matrix products, arithmetic and copies ran while one was open for 4% of the time, Pallas kernels for 35%

profile of v1, /device:TPU:0, one launch (start us, length us, event | category | flops | bytes accessed | tf_op | source)
XLA Modules:
  0.0 146.4 jit_solution(8529680566723515240)
XLA Ops:
  0.6 3.0 %collective-permute-start = (bf16[256,512]{1,0:T(8,128)(2,1)}, bf16[256,512]{1,0:T(8,128)(2,1)S(1)}, u32[]{:S(2)}, u32[]{:S(2)}) collective-permute-start(bf16[256,512]{1,0:T(8,128)(2,1)} %refs_0_.1), channel_id=1, source_target_pairs={{0,2},{1,3},{2,0},{3,1},{4,6},{5,7},{6,4},{7,5},{8,10},{9,11},{10,... | collective-permute-start | bytes 786440 | tf_op jit(solution)/shard_map/ppermute | solution.py:292
  3.6 1.5 %collective-permute-start.1 = (bf16[256,512]{1,0:T(8,128)(2,1)}, bf16[256,512]{1,0:T(8,128)(2,1)S(1)}, u32[]{:S(2)}, u32[]{:S(2)}) collective-permute-start(bf16[256,512]{1,0:T(8,128)(2,1)} %refs_0_.1), channel_id=1, source_target_pairs={{0,4},{1,5},{2,6},{3,7},{4,0},{5,1},{6,2},{7,3},{8,12},{9,13},{10,... | collective-permute-start | bytes 786440 | tf_op jit(solution)/shard_map/ppermute | solution.py:292
  5.2 0.0 collective-permute-start.2
  5.2 2.0 %collective-permute-start.7 = (bf16[512,512]{1,0:T(8,128)(2,1)}, bf16[512,512]{1,0:T(8,128)(2,1)S(1)}, u32[]{:S(2)}, u32[]{:S(2)}) collective-permute-start(bf16[512,512]{1,0:T(8,128)(2,1)} %second_ref.1), channel_id=1, source_target_pairs={{8,0},{16,24},{0,8},{24,16},{9,1},{17,25},{1,9},{25,17},{10,2},{18... | collective-permute-start | bytes 1572872 | tf_op jit(solution)/shard_map/ppermute | solution.py:292
  7.2 0.7 convert_element_type.49
  7.9 0.1 copy.13
  8.0 0.1 pad_add_fusion.1.base_ref
  8.1 0.1 pad.4.clone
  8.1 0.1 broadcast_in_dim.17
  8.2 0.8 maximum_maximum_fusion.aux_ref
  9.0 0.7 fusion.6
  9.7 0.7 maximum_bitcast_fusion.index_ref
  10.4 13.5 %order_counts.3 = (bf16[2048,1024]{1,0:T(8,128)(2,1)S(1)}, f32[16,1024]{1,0:T(8,128)S(1)}) custom-call(s32[2]{0:T(128)S(1)} %pad_add_fusion.1.base_ref, f32[128,128]{1,0:T(8,128)S(1)} %maximum_bitcast_fusion.index_ref, f32[16,2048]{1,0:T(8,128)S(1)} %maximum_maximum_fusion.aux_ref, s32[2048,2048]{1,0:T(8,128)} %count_ref.3), custom_call_target="tpu_custom_call" | custom-call | flops 8589934592 | bytes 16777216 | tf_op jit(solution)/shard_map/order_counts/pallas_call | solution.py:112
  23.9 2.0 %copy-done.2 = bf16[2048,1024]{1,0:T(8,128)(2,1)} copy-done((bf16[2048,1024]{1,0:T(8,128)(2,1)}, bf16[2048,1024]{1,0:T(8,128)(2,1)S(1)}, u32[]{:S(2)}) %copy-start.2) | copy-done | bytes 4194328
  25.9 0.1 pad_add_fusion.base_ref
  26.0 0.0 collective-permute-done.refs_1_
  26.0 0.8 collective-permute-start.10
  26.8 0.3 collective-permute-start.4
  27.1 0.0 collective-permute-done.2.refs_3_
  27.1 0.3 collective-permute-start.5
  27.4 0.7 copy-done.6
  28.1 0.2 collective-permute-start.6
  28.3 0.0 collective-permute-done.7.first_ref.second_ref
  28.4 0.7 collective-permute-start.8
  29.0 13.5 %order_counts.2 = (bf16[2048,1024]{1,0:T(8,128)(2,1)S(1)}, f32[16,1024]{1,0:T(8,128)S(1)}) custom-call(s32[2]{0:T(128)S(1)} %pad_add_fusion.base_ref, f32[128,128]{1,0:T(8,128)S(1)} %maximum_bitcast_fusion.index_ref, f32[16,2048]{1,0:T(8,128)S(1)} %maximum_maximum_fusion.aux_ref, s32[2048,2048]{1,0:T(8,128)} %count_ref.3), custom_call_target="tpu_custom_call" | custom-call | flops 8589934592 | bytes 16777216 | tf_op jit(solution)/shard_map/order_counts/pallas_call | solution.py:112
  42.5 2.0 %copy-done = bf16[2048,1024]{1,0:T(8,128)(2,1)} copy-done((bf16[2048,1024]{1,0:T(8,128)(2,1)}, bf16[2048,1024]{1,0:T(8,128)(2,1)S(1)}, u32[]{:S(2)}) %copy-start) | copy-done | bytes 4194328
  44.6 1.5 %collective-permute-start.11 = (bf16[512,512]{1,0:T(8,128)(2,1)S(1)}, bf16[512,512]{1,0:T(8,128)(2,1)S(1)}, u32[]{:S(2)}, u32[]{:S(2)}) collective-permute-start(bf16[512,512]{1,0:T(8,128)(2,1)S(1)} %collective-permute-done.10.second_ref), channel_id=1, source_target_pairs={{8,0},{16,24},{9,1},{17,25},{10,2},{18,26},{11,3},{19,27},{12,4},{... | collective-permute-start | bytes 1572872 | tf_op jit(solution)/shard_map/ppermute | solution.py:292
  46.1 0.0 collective-permute-done.4.refs_5_
  46.1 0.0 collective-permute-done.5.refs_6_
  46.2 0.0 copy-start.7
  46.2 0.9 copy-done.7
  47.1 5.7 %take_rows.1 = (bf16[2048,512]{1,0:T(8,128)(2,1)S(1)}, f32[2048,128]{1,0:T(8,128)S(1)}) custom-call(f32[128,128]{1,0:T(8,128)S(1)} %maximum_bitcast_fusion.index_ref, bf16[256,512]{1,0:T(8,128)(2,1)S(1)} %copy-done.5, bf16[256,512]{1,0:T(8,128)(2,1)S(1)} %collective-permute-done.refs_1_, bf16[256,512]{1,0:T(8,128)(2,1)S(1)} %collective-permute-done.1.refs_2_, ...), custom_call_target="tpu_custom_call" | custom-call | flops 4294967296 | bytes 4194304 | tf_op jit(solution)/shard_map/take_rows/pallas_call | solution.py:152
  52.8 0.0 collective-permute-done.8.second_ref
  52.8 1.5 %collective-permute-start.9 = (bf16[512,512]{1,0:T(8,128)(2,1)S(1)}, bf16[512,512]{1,0:T(8,128)(2,1)S(1)}, u32[]{:S(2)}, u32[]{:S(2)}) collective-permute-start(bf16[512,512]{1,0:T(8,128)(2,1)S(1)} %collective-permute-done.8.second_ref), channel_id=1, source_target_pairs={{8,0},{16,24},{9,1},{17,25},{10,2},{18,26},{11,3},{19,27},{12,4},{... | collective-permute-start | bytes 1572872 | tf_op jit(solution)/shard_map/ppermute | solution.py:292
  54.3 7.1 %cells.4 = (f32[2048,512]{1,0:T(8,128)S(1)}, f32[512,512]{1,0:T(8,128)S(1)}, bf16[512,512]{1,0:T(8,128)(2,1)S(1)}) custom-call(s32[1]{0:T(128)} %bitcast.1.pick_ref, bf16[512,512]{1,0:T(8,128)(2,1)S(1)} %collective-permute-done.7.first_ref.second_ref, bf16[512,512]{1,0:T(8,128)(2,1)S(1)} %collective-permute-done.10.second_ref, ...), custom_call_target="tpu_custom_call" | custom-call | flops 3221225472 | bytes 12582912 | tf_op jit(solution)/shard_map/cells/pallas_call | solution.py:251
  61.4 3.0 %collective-permute-done.11.first_ref = bf16[512,512]{1,0:T(8,128)(2,1)S(1)} collective-permute-done((bf16[512,512]{1,0:T(8,128)(2,1)S(1)}, bf16[512,512]{1,0:T(8,128)(2,1)S(1)}, u32[]{:S(2)}, u32[]{:S(2)}) %collective-permute-start.11) | collective-permute-done | bytes 524320 | tf_op jit(solution)/shard_map/ppermute | solution.py:292
  64.4 7.2 %cells.5 = (f32[2048,512]{1,0:T(8,128)S(1)}, f32[512,512]{1,0:T(8,128)S(1)}, bf16[512,512]{1,0:T(8,128)(2,1)S(1)}) custom-call(s32[1]{0:T(128)} %bitcast.1.pick_ref, bf16[512,512]{1,0:T(8,128)(2,1)S(1)} %collective-permute-done.11.first_ref, bf16[512,512]{1,0:T(8,128)(2,1)S(1)} %collective-permute-done.7.first_ref.second_ref, ...), custom_call_target="tpu_custom_call", output_to_operand_aliasing={{0}: (7, {})} | custom-call | flops 3221225472 | bytes 12582912 | tf_op jit(solution)/shard_map/cells/pallas_call | solution.py:251
  71.6 3.7 %collective-permute-done.9.first_ref = bf16[512,512]{1,0:T(8,128)(2,1)S(1)} collective-permute-done((bf16[512,512]{1,0:T(8,128)(2,1)S(1)}, bf16[512,512]{1,0:T(8,128)(2,1)S(1)}, u32[]{:S(2)}, u32[]{:S(2)}) %collective-permute-start.9) | collective-permute-done | bytes 524320 | tf_op jit(solution)/shard_map/ppermute | solution.py:292
  75.3 7.2 %cells.6 = (f32[2048,512]{1,0:T(8,128)S(1)}, f32[512,512]{1,0:T(8,128)S(1)}, bf16[512,512]{1,0:T(8,128)(2,1)S(1)}) custom-call(s32[1]{0:T(128)} %bitcast.1.pick_ref, bf16[512,512]{1,0:T(8,128)(2,1)S(1)} %collective-permute-done.9.first_ref, bf16[512,512]{1,0:T(8,128)(2,1)S(1)} %collective-permute-done.8.second_ref, ...), custom_call_target="tpu_custom_call", output_to_operand_aliasing={{0}: (7, {})} | custom-call | flops 3221225472 | bytes 12582912 | tf_op jit(solution)/shard_map/cells/pallas_call | solution.py:251
  82.5 8.1 %cells.7 = (f32[2048,512]{1,0:T(8,128)S(1)}, f32[512,512]{1,0:T(8,128)S(1)}, bf16[512,512]{1,0:T(8,128)(2,1)}) custom-call(s32[1]{0:T(128)} %bitcast.1.pick_ref, bf16[512,512]{1,0:T(8,128)(2,1)S(1)} %copy-done.4, bf16[512,512]{1,0:T(8,128)(2,1)S(1)} %copy-done.4, bf16[2048,512]{1,0:T(8,128)(2,1)S(1)} %get-tuple-element.19.wvec_ref, ...), custom_call_target="tpu_custom_call", output_to_operand_aliasing={{0}: (7, {})} | custom-call | flops 3221225472 | bytes 12582912 | tf_op jit(solution)/shard_map/cells/pallas_call | solution.py:251
  90.6 4.6 %put_rows.3 = f32[4,256,512]{2,1,0:T(8,128)S(1)} custom-call(f32[1,2048]{1,0:T(1,128)S(1)} %bitcast.26, f32[2048,512]{1,0:T(8,128)S(1)} %get-tuple-element.28.grad_ref), custom_call_target="tpu_custom_call" | custom-call | flops 4294967296 | bytes 6291456 | tf_op jit(solution)/shard_map/put_rows/pallas_call | solution.py:282
  95.2 0.1 collective-permute-start.12
  95.3 1.5 %collective-permute-start.19 = (bf16[512,512]{1,0:T(8,128)(2,1)S(1)}, bf16[512,512]{1,0:T(8,128)(2,1)S(1)}, u32[]{:S(2)}, u32[]{:S(2)}) collective-permute-start(bf16[512,512]{1,0:T(8,128)(2,1)S(1)} %get-tuple-element.35), channel_id=1, source_target_pairs={{0,8},{24,16},{1,9},{25,17},{2,10},{26,18},{3,11},{27,19},{4,12},{... | collective-permute-start | bytes 1572872 | tf_op jit(solution)/shard_map/ppermute | solution.py:292
  96.8 1.3 collective-permute-start.17
  98.1 1.3 collective-permute-start.16
  99.4 9.5 %collective-permute-done.19 = bf16[512,512]{1,0:T(8,128)(2,1)S(1)} collective-permute-done((bf16[512,512]{1,0:T(8,128)(2,1)S(1)}, bf16[512,512]{1,0:T(8,128)(2,1)S(1)}, u32[]{:S(2)}, u32[]{:S(2)}) %collective-permute-start.19) | collective-permute-done | bytes 524320 | tf_op jit(solution)/shard_map/ppermute | solution.py:292
  108.9 0.2 add_convert_fusion.1
  109.1 0.7 collective-permute-start.20
  109.8 10.3 %collective-permute-done.17 = bf16[512,512]{1,0:T(8,128)(2,1)S(1)} collective-permute-done((bf16[512,512]{1,0:T(8,128)(2,1)S(1)}, bf16[512,512]{1,0:T(8,128)(2,1)S(1)}, u32[]{:S(2)}, u32[]{:S(2)}) %collective-permute-start.17) | collective-permute-done | bytes 524320 | tf_op jit(solution)/shard_map/ppermute | solution.py:292
  120.2 0.2 add_convert_fusion.2
  120.3 0.9 collective-permute-start.18
  121.3 4.6 %put_rows.2 = f32[4,256,512]{2,1,0:T(8,128)S(1)} custom-call(f32[1,2048]{1,0:T(1,128)S(1)} %bitcast.27, f32[2048,512]{1,0:T(8,128)S(1)} %get-tuple-element.28.grad_ref), custom_call_target="tpu_custom_call" | custom-call | flops 4294967296 | bytes 6291456 | tf_op jit(solution)/shard_map/put_rows/pallas_call | solution.py:282
  125.9 0.2 add_convert_fusion
  126.1 1.3 collective-permute-start.21
  127.4 0.5 fusion.11
  127.9 0.1 slice_bitcast_fusion.3
  128.0 1.6 %collective-permute-start.13 = (bf16[256,512]{1,0:T(8,128)(2,1)S(1)}, bf16[256,512]{1,0:T(8,128)(2,1)S(1)}, u32[]{:S(2)}, u32[]{:S(2)}) collective-permute-start(bf16[256,512]{1,0:T(8,128)(2,1)S(1)} %get-tuple-element.38), channel_id=1, source_target_pairs={{0,2},{1,3},{2,0},{3,1},{4,6},{5,7},{6,4},{7,5},{8,10},{9,11},{10,... | collective-permute-start | bytes 786440 | tf_op jit(solution)/shard_map/ppermute | solution.py:292
  129.5 1.5 %collective-permute-start.14 = (bf16[256,512]{1,0:T(8,128)(2,1)S(1)}, bf16[256,512]{1,0:T(8,128)(2,1)S(1)}, u32[]{:S(2)}, u32[]{:S(2)}) collective-permute-start(bf16[256,512]{1,0:T(8,128)(2,1)S(1)} %get-tuple-element.40), channel_id=1, source_target_pairs={{0,4},{1,5},{2,6},{3,7},{4,0},{5,1},{6,2},{7,3},{8,12},{9,13},{10,... | collective-permute-start | bytes 786440 | tf_op jit(solution)/shard_map/ppermute | solution.py:292
  131.1 0.1 collective-permute-done.16
  131.1 2.4 %collective-permute-start.15 = (bf16[256,512]{1,0:T(8,128)(2,1)S(1)}, bf16[256,512]{1,0:T(8,128)(2,1)S(1)}, u32[]{:S(2)}, u32[]{:S(2)}) collective-permute-start(bf16[256,512]{1,0:T(8,128)(2,1)S(1)} %get-tuple-element.39), channel_id=1, source_target_pairs={{0,6},{1,7},{2,4},{3,5},{4,2},{5,3},{6,0},{7,1},{8,14},{9,15},{10,... | collective-permute-start | bytes 786440 | tf_op jit(solution)/shard_map/ppermute | solution.py:292
  133.6 10.6 %collective-permute-done.21 = bf16[512,512]{1,0:T(8,128)(2,1)S(1)} collective-permute-done((bf16[512,512]{1,0:T(8,128)(2,1)S(1)}, bf16[512,512]{1,0:T(8,128)(2,1)S(1)}, u32[]{:S(2)}, u32[]{:S(2)}) %collective-permute-start.21) | collective-permute-done | bytes 524320 | tf_op jit(solution)/shard_map/ppermute | solution.py:292
  144.2 1.3 add_multiply_fusion
  145.5 0.0 collective-permute-done.13
  145.5 0.9 fusion.3
  (23 shorter events, 0.1 us)
Async XLA Ops:
  0.6 25.4 %collective-permute-start = (bf16[256,512]{1,0:T(8,128)(2,1)}, bf16[256,512]{1,0:T(8,128)(2,1)S(1)}, u32[]{:S(2)}, u32[]{:S(2)}) collective-permute-start(bf16[256,512]{1,0:T(8,128)(2,1)} %refs_0_.1), channel_id=1, source_target_pairs={{0,2},{1,3},{2,0},{3,1},{4,6},{5,7},{6,4},{7,5},{8,10},{9,11},{10,... | collective-permute-start | bytes 786440 | tf_op jit(solution)/shard_map/ppermute | solution.py:292
  3.6 23.2 %collective-permute-start.1 = (bf16[256,512]{1,0:T(8,128)(2,1)}, bf16[256,512]{1,0:T(8,128)(2,1)S(1)}, u32[]{:S(2)}, u32[]{:S(2)}) collective-permute-start(bf16[256,512]{1,0:T(8,128)(2,1)} %refs_0_.1), channel_id=1, source_target_pairs={{0,4},{1,5},{2,6},{3,7},{4,0},{5,1},{6,2},{7,3},{8,12},{9,13},{10,... | collective-permute-start | bytes 786440 | tf_op jit(solution)/shard_map/ppermute | solution.py:292
  5.2 22.0 %collective-permute-start.2 = (bf16[256,512]{1,0:T(8,128)(2,1)}, bf16[256,512]{1,0:T(8,128)(2,1)S(1)}, u32[]{:S(2)}, u32[]{:S(2)}) collective-permute-start(bf16[256,512]{1,0:T(8,128)(2,1)} %refs_0_.1), channel_id=1, source_target_pairs={{0,6},{1,7},{2,4},{3,5},{4,2},{5,3},{6,0},{7,1},{8,14},{9,15},{10,... | collective-permute-start | bytes 786440 | tf_op jit(solution)/shard_map/ppermute | solution.py:292
  5.2 22.2 %collective-permute-start.3 = (bf16[256,512]{1,0:T(8,128)(2,1)}, bf16[256,512]{1,0:T(8,128)(2,1)S(1)}, u32[]{:S(2)}, u32[]{:S(2)}) collective-permute-start(bf16[256,512]{1,0:T(8,128)(2,1)} %refs_0_.1), channel_id=1, source_target_pairs={{0,1},{1,0},{2,3},{3,2},{4,5},{5,4},{6,7},{7,6},{8,9},{9,8},{10,11... | collective-permute-start | bytes 786440 | tf_op jit(solution)/shard_map/ppermute | solution.py:292
  5.2 23.2 %collective-permute-start.7 = (bf16[512,512]{1,0:T(8,128)(2,1)}, bf16[512,512]{1,0:T(8,128)(2,1)S(1)}, u32[]{:S(2)}, u32[]{:S(2)}) collective-permute-start(bf16[512,512]{1,0:T(8,128)(2,1)} %second_ref.1), channel_id=1, source_target_pairs={{8,0},{16,24},{0,8},{24,16},{9,1},{17,25},{1,9},{25,17},{10,2},{18... | collective-permute-start | bytes 1572872 | tf_op jit(solution)/shard_map/ppermute | solution.py:292
  10.4 15.6 %copy-start.4 = (bf16[512,512]{1,0:T(8,128)(2,1)S(1)}, bf16[512,512]{1,0:T(8,128)(2,1)}, u32[]{:S(2)}) copy-start(bf16[512,512]{1,0:T(8,128)(2,1)} %second_ref.1) | copy-start | bytes 1572868
  23.9 2.0 %copy-start.2 = (bf16[2048,1024]{1,0:T(8,128)(2,1)}, bf16[2048,1024]{1,0:T(8,128)(2,1)S(1)}, u32[]{:S(2)}) copy-start(bf16[2048,1024]{1,0:T(8,128)(2,1)S(1)} %get-tuple-element.23.count_ref) | copy-start | bytes 12582916
  26.0 20.2 %copy-start.5 = (bf16[256,512]{1,0:T(8,128)(2,1)S(1)}, bf16[256,512]{1,0:T(8,128)(2,1)}, u32[]{:S(2)}) copy-start(bf16[256,512]{1,0:T(8,128)(2,1)} %refs_0_.1) | copy-start | bytes 786436
  26.0 18.6 %collective-permute-start.10 = (bf16[512,512]{1,0:T(8,128)(2,1)S(1)}, bf16[512,512]{1,0:T(8,128)(2,1)S(1)}, u32[]{:S(2)}, u32[]{:S(2)}) collective-permute-start(bf16[512,512]{1,0:T(8,128)(2,1)S(1)} %copy-done.4), channel_id=1, source_target_pairs={{8,16},{16,8},{9,17},{17,9},{10,18},{18,10},{11,19},{19,11},{12,20... | collective-permute-start | bytes 1572872 | tf_op jit(solution)/shard_map/ppermute | solution.py:292
  26.8 19.3 %collective-permute-start.4 = (bf16[256,512]{1,0:T(8,128)(2,1)S(1)}, bf16[256,512]{1,0:T(8,128)(2,1)}, u32[]{:S(2)}, u32[]{:S(2)}) collective-permute-start(bf16[256,512]{1,0:T(8,128)(2,1)S(1)} %collective-permute-done.refs_1_), channel_id=1, source_target_pairs={{0,1},{1,0},{2,3},{3,2},{4,5},{5,4},{6,7},{7,6},{8,9},{9,8},{10,11... | collective-permute-start | bytes 786440 | tf_op jit(solution)/shard_map/ppermute | solution.py:292
  27.1 19.0 %collective-permute-start.5 = (bf16[256,512]{1,0:T(8,128)(2,1)S(1)}, bf16[256,512]{1,0:T(8,128)(2,1)}, u32[]{:S(2)}, u32[]{:S(2)}) collective-permute-start(bf16[256,512]{1,0:T(8,128)(2,1)S(1)} %collective-permute-done.1.refs_2_), channel_id=1, source_target_pairs={{0,1},{1,0},{2,3},{3,2},{4,5},{5,4},{6,7},{7,6},{8,9},{9,8},{10,11... | collective-permute-start | bytes 786440 | tf_op jit(solution)/shard_map/ppermute | solution.py:292
  27.4 0.7 copy-start.6
  28.1 18.0 %collective-permute-start.6 = (bf16[256,512]{1,0:T(8,128)(2,1)S(1)}, bf16[256,512]{1,0:T(8,128)(2,1)}, u32[]{:S(2)}, u32[]{:S(2)}) collective-permute-start(bf16[256,512]{1,0:T(8,128)(2,1)S(1)} %collective-permute-done.2.refs_3_), channel_id=1, source_target_pairs={{0,1},{1,0},{2,3},{3,2},{4,5},{5,4},{6,7},{7,6},{8,9},{9,8},{10,11... | collective-permute-start | bytes 786440 | tf_op jit(solution)/shard_map/ppermute | solution.py:292
  28.4 24.5 %collective-permute-start.8 = (bf16[512,512]{1,0:T(8,128)(2,1)S(1)}, bf16[512,512]{1,0:T(8,128)(2,1)S(1)}, u32[]{:S(2)}, u32[]{:S(2)}) collective-permute-start(bf16[512,512]{1,0:T(8,128)(2,1)S(1)} %collective-permute-done.7.first_ref.second_ref), channel_id=1, source_target_pairs={{8,16},{16,8},{9,17},{17,9},{10,18},{18,10},{11,19},{19,11},{12,20... | collective-permute-start | bytes 1572872 | tf_op jit(solution)/shard_map/ppermute | solution.py:292
  42.5 2.0 %copy-start = (bf16[2048,1024]{1,0:T(8,128)(2,1)}, bf16[2048,1024]{1,0:T(8,128)(2,1)S(1)}, u32[]{:S(2)}) copy-start(bf16[2048,1024]{1,0:T(8,128)(2,1)S(1)} %get-tuple-element.20.count_ref) | copy-start | bytes 12582916
  44.6 9.8 %copy-start.3 = (bf16[2048,1024]{1,0:T(8,128)(2,1)S(1)}, bf16[2048,1024]{1,0:T(8,128)(2,1)}, u32[]{:S(2)}) copy-start(bf16[2048,1024]{1,0:T(8,128)(2,1)} %copy-done.2) | copy-start | bytes 12582916
  44.6 19.8 %collective-permute-start.11 = (bf16[512,512]{1,0:T(8,128)(2,1)S(1)}, bf16[512,512]{1,0:T(8,128)(2,1)S(1)}, u32[]{:S(2)}, u32[]{:S(2)}) collective-permute-start(bf16[512,512]{1,0:T(8,128)(2,1)S(1)} %collective-permute-done.10.second_ref), channel_id=1, source_target_pairs={{8,0},{16,24},{9,1},{17,25},{10,2},{18,26},{11,3},{19,27},{12,4},{... | collective-permute-start | bytes 1572872 | tf_op jit(solution)/shard_map/ppermute | solution.py:292
  46.2 1.0 copy-start.7
  52.8 22.5 %collective-permute-start.9 = (bf16[512,512]{1,0:T(8,128)(2,1)S(1)}, bf16[512,512]{1,0:T(8,128)(2,1)S(1)}, u32[]{:S(2)}, u32[]{:S(2)}) collective-permute-start(bf16[512,512]{1,0:T(8,128)(2,1)S(1)} %collective-permute-done.8.second_ref), channel_id=1, source_target_pairs={{8,0},{16,24},{9,1},{17,25},{10,2},{18,26},{11,3},{19,27},{12,4},{... | collective-permute-start | bytes 1572872 | tf_op jit(solution)/shard_map/ppermute | solution.py:292
  64.4 10.9 %copy-start.1 = (bf16[2048,1024]{1,0:T(8,128)(2,1)S(1)}, bf16[2048,1024]{1,0:T(8,128)(2,1)}, u32[]{:S(2)}) copy-start(bf16[2048,1024]{1,0:T(8,128)(2,1)} %copy-done) | copy-start | bytes 12582916
  95.2 32.2 %collective-permute-start.12 = (f32[4,256,512]{2,1,0:T(8,128)S(1)}, f32[4,256,512]{2,1,0:T(8,128)S(1)}, u32[]{:S(2)}, u32[]{:S(2)}) collective-permute-start(f32[4,256,512]{2,1,0:T(8,128)S(1)} %put_rows.3), channel_id=1, source_target_pairs={{0,1},{1,0},{2,3},{3,2},{4,5},{5,4},{6,7},{7,6},{8,9},{9,8},{10,11... | collective-permute-start | bytes 6291464 | tf_op jit(solution)/shard_map/ppermute | solution.py:292
  95.3 13.7 %collective-permute-start.19 = (bf16[512,512]{1,0:T(8,128)(2,1)S(1)}, bf16[512,512]{1,0:T(8,128)(2,1)S(1)}, u32[]{:S(2)}, u32[]{:S(2)}) collective-permute-start(bf16[512,512]{1,0:T(8,128)(2,1)S(1)} %get-tuple-element.35), channel_id=1, source_target_pairs={{0,8},{24,16},{1,9},{25,17},{2,10},{26,18},{3,11},{27,19},{4,12},{... | collective-permute-start | bytes 1572872 | tf_op jit(solution)/shard_map/ppermute | solution.py:292
  96.8 23.4 %collective-permute-start.17 = (bf16[512,512]{1,0:T(8,128)(2,1)S(1)}, bf16[512,512]{1,0:T(8,128)(2,1)S(1)}, u32[]{:S(2)}, u32[]{:S(2)}) collective-permute-start(bf16[512,512]{1,0:T(8,128)(2,1)S(1)} %get-tuple-element.32), channel_id=1, source_target_pairs={{0,8},{24,16},{1,9},{25,17},{2,10},{26,18},{3,11},{27,19},{4,12},{... | collective-permute-start | bytes 1572872 | tf_op jit(solution)/shard_map/ppermute | solution.py:292
  98.1 33.0 %collective-permute-start.16 = (bf16[512,512]{1,0:T(8,128)(2,1)S(1)}, bf16[512,512]{1,0:T(8,128)(2,1)S(1)}, u32[]{:S(2)}, u32[]{:S(2)}) collective-permute-start(bf16[512,512]{1,0:T(8,128)(2,1)S(1)} %get-tuple-element.30), channel_id=1, source_target_pairs={{0,8},{24,16},{1,9},{25,17},{2,10},{26,18},{3,11},{27,19},{4,12},{... | collective-permute-start | bytes 1572872 | tf_op jit(solution)/shard_map/ppermute | solution.py:292
  109.1 16.8 %collective-permute-start.20 = (bf16[512,512]{1,0:T(8,128)(2,1)S(1)}, bf16[512,512]{1,0:T(8,128)(2,1)S(1)}, u32[]{:S(2)}, u32[]{:S(2)}) collective-permute-start(bf16[512,512]{1,0:T(8,128)(2,1)S(1)} %add_convert_fusion.1), channel_id=1, source_target_pairs={{8,16},{16,8},{9,17},{17,9},{10,18},{18,10},{11,19},{19,11},{12,20... | collective-permute-start | bytes 1572872 | tf_op jit(solution)/shard_map/ppermute | solution.py:292
  120.3 13.2 %collective-permute-start.18 = (bf16[512,512]{1,0:T(8,128)(2,1)S(1)}, bf16[512,512]{1,0:T(8,128)(2,1)S(1)}, u32[]{:S(2)}, u32[]{:S(2)}) collective-permute-start(bf16[512,512]{1,0:T(8,128)(2,1)S(1)} %add_convert_fusion.2), channel_id=1, source_target_pairs={{8,16},{16,8},{9,17},{17,9},{10,18},{18,10},{11,19},{19,11},{12,20... | collective-permute-start | bytes 1572872 | tf_op jit(solution)/shard_map/ppermute | solution.py:292
  126.1 18.1 %collective-permute-start.21 = (bf16[512,512]{1,0:T(8,128)(2,1)S(1)}, bf16[512,512]{1,0:T(8,128)(2,1)S(1)}, u32[]{:S(2)}, u32[]{:S(2)}) collective-permute-start(bf16[512,512]{1,0:T(8,128)(2,1)S(1)} %add_convert_fusion), channel_id=1, source_target_pairs={{8,0},{16,24},{9,1},{17,25},{10,2},{18,26},{11,3},{19,27},{12,4},{... | collective-permute-start | bytes 1572872 | tf_op jit(solution)/shard_map/ppermute | solution.py:292
  128.0 17.5 %collective-permute-start.13 = (bf16[256,512]{1,0:T(8,128)(2,1)S(1)}, bf16[256,512]{1,0:T(8,128)(2,1)S(1)}, u32[]{:S(2)}, u32[]{:S(2)}) collective-permute-start(bf16[256,512]{1,0:T(8,128)(2,1)S(1)} %get-tuple-element.38), channel_id=1, source_target_pairs={{0,2},{1,3},{2,0},{3,1},{4,6},{5,7},{6,4},{7,5},{8,10},{9,11},{10,... | collective-permute-start | bytes 786440 | tf_op jit(solution)/shard_map/ppermute | solution.py:292
  129.5 15.9 %collective-permute-start.14 = (bf16[256,512]{1,0:T(8,128)(2,1)S(1)}, bf16[256,512]{1,0:T(8,128)(2,1)S(1)}, u32[]{:S(2)}, u32[]{:S(2)}) collective-permute-start(bf16[256,512]{1,0:T(8,128)(2,1)S(1)} %get-tuple-element.40), channel_id=1, source_target_pairs={{0,4},{1,5},{2,6},{3,7},{4,0},{5,1},{6,2},{7,3},{8,12},{9,13},{10,... | collective-permute-start | bytes 786440 | tf_op jit(solution)/shard_map/ppermute | solution.py:292
  131.1 14.3 %collective-permute-start.15 = (bf16[256,512]{1,0:T(8,128)(2,1)S(1)}, bf16[256,512]{1,0:T(8,128)(2,1)S(1)}, u32[]{:S(2)}, u32[]{:S(2)}) collective-permute-start(bf16[256,512]{1,0:T(8,128)(2,1)S(1)} %get-tuple-element.39), channel_id=1, source_target_pairs={{0,6},{1,7},{2,4},{3,5},{4,2},{5,3},{6,0},{7,1},{8,14},{9,15},{10,... | collective-permute-start | bytes 786440 | tf_op jit(solution)/shard_map/ppermute | solution.py:292
